TPU v7x, 32 devices: a whole 2x2x4 slice. The times are simulated.
32 devices in a mesh: row: 8 (over z, x), col: 4 (over y, core).
Axes of the slice: x: 2, y: 2, z: 4, core: 2. Of those that a mesh axis runs over, the one named last changes fastest.
Arguments:
- trailing: float32 [16, 4, 512, 512], P('row', 'col'), may hold values from -6 to 6
- panel_block: float32 [16, 512, 1024], P('row', 'col'), may hold values from -2.5 to 2.5
- diag_block: float32 [1024, 1024], P('row'), as said below
- tile_map: int32 [16], replicated, may hold values from 0 to 15, each once
Outputs:
- updated_trailing: float32 [16, 4, 512, 512], P('row', 'col')
- panel_factor: float32 [16, 512, 1024], P('row', 'col')
- diag_factor: float32 [1024, 1024], P('row')
Inputs may be any that keep to these rules, and one draw needn't show every extreme that they name: `tile_map`: each of the 16 trailing tile rows stands in exactly one slot. `diag_block`: symmetric and positive definite.
All inputs are finite; a program needn't handle non-finite values.
Results may differ from a plain program's by a relative error of at most 0.0003.
Values sent between devices are 32-bit elements; how exact they have to be, the bound alone decides.
No kernel may reach another device: no remote copies, remote signals or barrier semaphores. Data moves between devices by JAX's collectives and lax.ppermute only.
A program may use at most 128 MiB of HBM per device.

v0:
```python
import jax
import jax.numpy as jnp
from jax import lax
from jax.sharding import PartitionSpec as P


def spread(block, axis, source):
    block = jnp.where(lax.axis_index(axis) == source, block, jnp.zeros_like(block))
    return lax.psum(block, axis)


def solve_rows(factor, row_block):
    flattened = row_block.reshape(-1, row_block.shape[-1])
    solved = lax.linalg.triangular_solve(
        factor, flattened, left_side=False, lower=True, transpose_a=True
    )
    return solved.reshape(row_block.shape)


def per_device(trailing, panel_block, diag_block, tile_map):
    slot_count = trailing.shape[0]
    whole_diag = lax.all_gather(diag_block, "row", axis=0, tiled=True)
    factor = jnp.linalg.cholesky(whole_diag)
    row_rank = lax.axis_index("row")
    column = lax.axis_index("col")
    slot_index = jnp.arange(tile_map.shape[0], dtype=jnp.int32)
    owner_slot = jnp.sum(jnp.where(tile_map == column, slot_index, 0))
    owner_row = owner_slot // slot_count
    local_slot = owner_slot % slot_count
    own_tiles = lax.dynamic_slice_in_dim(tile_map, row_rank * slot_count, slot_count)
    own_piece = solve_rows(factor, panel_block)
    row_panels = lax.all_gather(own_piece, "col", axis=1, tiled=True)
    offered = lax.dynamic_index_in_dim(row_panels, local_slot, 0, keepdims=False)
    column_panel = spread(offered, "row", owner_row)
    products = jnp.einsum("tak,bk->tab", row_panels, column_panel, precision=lax.Precision.HIGHEST)
    tile_live = own_tiles >= column
    current = trailing[:, 0]
    updated = jnp.where(tile_live[:, None, None], current - products, jnp.zeros_like(current))
    diag_rows = diag_block.shape[0]
    diag_piece = lax.dynamic_slice_in_dim(factor, row_rank * diag_rows, diag_rows, 0)
    return (updated[:, None], own_piece, diag_piece)


def solution(mesh):
    in_specs = (P("row", "col", None, None), P("row", "col", None), P("row", None), P())
    out_specs = (P("row", "col", None, None), P("row", "col", None), P("row", None))
    return jax.shard_map(
        per_device, mesh=mesh, in_specs=in_specs, out_specs=out_specs, check_vma=False
    )
```

profile of v0, /device:TPU:0, one launch (start us, length us, event | category | flops | bytes accessed | tf_op | source)
XLA Modules:
  0.0 586.2 jit_solution(14081571354756634575)
XLA Ops:
  7.2 2.0 copy.7
  9.3 79.0 %all-gather.3.cloned.1.call-done = f32[1024,1024]{0,1:T(8,128)} async-done(((f32[128,1024]{0,1:T(8,128)}), f32[1024,1024]{0,1:T(8,128)}) %all-gather.3.cloned.1.call-update) | async-done | bytes 4194320 | tf_op jit(solution)/shard_map/all_gather | solution.py:22
  88.4 5.3 copy.8
  93.7 4.4 fusion
  98.1 1.9 copy-done
  100.1 11.7 %cholesky.223 = f32[128,128]{1,0:T(8,128)S(1)} custom-call(f32[128,128]{1,0:T(8,128)S(1)} %cholesky.580), custom_call_target="Cholesky" | custom-call | tf_op jit(solution)/shard_map/jit(cholesky)/cholesky | solution.py:23
  111.8 9.8 %custom-call.62 = f32[1,128,128]{1,2,0:T(8,128)S(1)} custom-call(f32[1,128,128]{2,1,0:T(8,128)S(1)} %get-tuple-element.72), custom_call_target="InvertDiagBlocksLowerTriangular" | custom-call | tf_op jit(solution)/shard_map/jit(cholesky)/cholesky | solution.py:23
  121.6 2.5 cholesky.255
  124.1 2.3 constant_dynamic-update-slice_fusion.32
  128.0 11.9 %cholesky.244 = f32[128,128]{1,0:T(8,128)S(1)} custom-call(f32[128,128]{1,0:T(8,128)S(1)} %cholesky.584), custom_call_target="Cholesky" | custom-call | tf_op jit(solution)/shard_map/jit(cholesky)/cholesky | solution.py:23
  140.6 9.8 %custom-call.63 = f32[1,128,128]{1,2,0:T(8,128)S(1)} custom-call(f32[1,128,128]{2,1,0:T(8,128)S(1)} %get-tuple-element.69), custom_call_target="InvertDiagBlocksLowerTriangular" | custom-call | tf_op jit(solution)/shard_map/jit(cholesky)/cholesky | solution.py:23
  151.6 2.1 convolution_subtract_fusion.1
  153.7 11.7 %cholesky.468 = f32[128,128]{1,0:T(8,128)S(1)} custom-call(f32[128,128]{1,0:T(8,128)S(1)} %cholesky.589), custom_call_target="Cholesky" | custom-call | tf_op jit(solution)/shard_map/jit(cholesky)/cholesky | solution.py:23
  166.7 9.8 %custom-call.64 = f32[1,128,128]{1,2,0:T(8,128)S(1)} custom-call(f32[1,128,128]{2,1,0:T(8,128)S(1)} %get-tuple-element.66), custom_call_target="InvertDiagBlocksLowerTriangular" | custom-call | tf_op jit(solution)/shard_map/jit(cholesky)/cholesky | solution.py:23
  177.7 2.3 convolution_subtract_fusion.2
  180.1 11.9 %cholesky.487 = f32[128,128]{1,0:T(8,128)S(1)} custom-call(f32[128,128]{1,0:T(8,128)S(1)} %cholesky.594), custom_call_target="Cholesky" | custom-call | tf_op jit(solution)/shard_map/jit(cholesky)/cholesky | solution.py:23
  193.3 9.8 %custom-call.65 = f32[1,128,128]{1,2,0:T(8,128)S(1)} custom-call(f32[1,128,128]{2,1,0:T(8,128)S(1)} %get-tuple-element.63), custom_call_target="InvertDiagBlocksLowerTriangular" | custom-call | tf_op jit(solution)/shard_map/jit(cholesky)/cholesky | solution.py:23
  204.2 2.3 convolution_subtract_fusion.3
  206.5 11.7 %cholesky.506 = f32[128,128]{1,0:T(8,128)S(1)} custom-call(f32[128,128]{1,0:T(8,128)S(1)} %cholesky.599), custom_call_target="Cholesky" | custom-call | tf_op jit(solution)/shard_map/jit(cholesky)/cholesky | solution.py:23
  219.6 10.2 %custom-call.66 = f32[1,128,128]{1,2,0:T(8,128)S(1)} custom-call(f32[1,128,128]{2,1,0:T(8,128)S(1)} %get-tuple-element.60), custom_call_target="InvertDiagBlocksLowerTriangular" | custom-call | tf_op jit(solution)/shard_map/jit(cholesky)/cholesky | solution.py:23
  230.8 2.3 convolution_subtract_fusion.4
  233.1 11.7 %cholesky.526 = f32[128,128]{1,0:T(8,128)S(1)} custom-call(f32[128,128]{1,0:T(8,128)S(1)} %cholesky.604), custom_call_target="Cholesky" | custom-call | tf_op jit(solution)/shard_map/jit(cholesky)/cholesky | solution.py:23
  246.1 9.8 %custom-call.67 = f32[1,128,128]{1,2,0:T(8,128)S(1)} custom-call(f32[1,128,128]{2,1,0:T(8,128)S(1)} %get-tuple-element.57), custom_call_target="InvertDiagBlocksLowerTriangular" | custom-call | tf_op jit(solution)/shard_map/jit(cholesky)/cholesky | solution.py:23
  256.9 2.0 convolution_subtract_fusion.11
  258.9 11.9 %cholesky.546 = f32[128,128]{1,0:T(8,128)S(1)} custom-call(f32[128,128]{1,0:T(8,128)S(1)} %cholesky.609), custom_call_target="Cholesky" | custom-call | tf_op jit(solution)/shard_map/jit(cholesky)/cholesky | solution.py:23
  272.0 9.8 %custom-call.68 = f32[1,128,128]{1,2,0:T(8,128)S(1)} custom-call(f32[1,128,128]{2,1,0:T(8,128)S(1)} %get-tuple-element.54), custom_call_target="InvertDiagBlocksLowerTriangular" | custom-call | tf_op jit(solution)/shard_map/jit(cholesky)/cholesky | solution.py:23
  282.7 1.8 convolution_subtract_fusion.13
  284.5 11.7 %cholesky.564 = f32[128,128]{1,0:T(8,128)S(1)} custom-call(f32[128,128]{1,0:T(8,128)S(1)} %convolution_subtract_fusion.13), custom_call_target="Cholesky" | custom-call | tf_op jit(solution)/shard_map/jit(cholesky)/cholesky | solution.py:23
  303.2 6.7 %fusion.1 = (f32[1024,1024]{1,0:T(8,128)}, f32[1024,1024]{1,0:T(8,128)}) fusion(f32[1024,1024]{1,0:T(8,128)} %get-tuple-element.52, pred[]{:T(512)S(6)} %cholesky.579), kind=kLoop, calls=%fused_computation.6 | loop fusion | flops 4194304 | bytes 12582913 | tf_op jit(solution)/shard_map/triangular_solve | solution.py:14
  309.9 23.2 %while.1 = (s32[]{:T(128)}, f32[1024,1024]{1,0:T(8,128)}, s32[8,2]{0,1:T(2,128)S(1)}, f32[8,128,128]{2,1,0:T(8,128)S(1)}, s32[]{:T(128)}) while((s32[]{:T(128)}, f32[1024,1024]{1,0:T(8,128)}, s32[8,2]{0,1:T(2,128)S(1)}, f32[8,128,128]{2,1,0:T(8,128)S(1)}, s32[]{:T(128)}) %tuple.63), condition=%wide.while_cond, body=%wide.while_body.sunk | while | flops 2 | bytes 131189 | solution.py:14
  310.5 2.3 bitcast_dynamic-update-slice_fusion.2
  313.4 2.3 bitcast_dynamic-update-slice_fusion.2
  316.3 2.3 bitcast_dynamic-update-slice_fusion.2
  319.2 2.3 bitcast_dynamic-update-slice_fusion.2
  322.1 2.3 bitcast_dynamic-update-slice_fusion.2
  325.1 2.3 bitcast_dynamic-update-slice_fusion.2
  328.0 2.3 bitcast_dynamic-update-slice_fusion.2
  330.9 2.2 bitcast_dynamic-update-slice_fusion.2
  333.1 78.8 %custom-call.69 = f32[8,128,128]{1,2,0:T(8,128)S(1)} custom-call(f32[8,128,128]{2,1,0:T(8,128)S(1)} %get-tuple-element.10), custom_call_target="InvertDiagBlocksLowerTriangular" | custom-call | tf_op jit(solution)/shard_map/triangular_solve | solution.py:14
  417.8 2.0 convolution_subtract_fusion.6
  420.1 2.2 convolution_subtract_fusion.5
  422.7 2.4 convolution_subtract_fusion.9
  425.4 2.7 convolution_subtract_fusion.12
  433.1 29.5 %all-gather.5.cloned.1.call-done = f32[2,512,1024]{2,1,0:T(8,128)} async-done(((f32[2,128,1024]{2,1,0:T(8,128)}), f32[2,512,1024]{2,1,0:T(8,128)}) %all-gather.5.cloned.1.call-update) | async-done | bytes 4194320 | tf_op jit(solution)/shard_map/all_gather | solution.py:32
  462.6 3.2 select_bitcast_fusion
  465.9 1.9 constant_dynamic-slice_fusion.1
  467.8 100.9 %all-reduce.3.cloned.1.call-done = f32[512,1024]{1,0:T(8,128)} async-done(((f32[512,1024]{1,0:T(8,128)}), f32[512,1024]{1,0:T(8,128)}) %all-reduce.3.cloned.1.call-update) | async-done | bytes 2097168 | tf_op jit(solution)/shard_map/psum | solution.py:9
  568.7 10.7 %fusion.5 = f32[2,1,512,512]{3,2,1,0:T(8,128)} fusion(f32[2,1,512,512]{3,2,1,0:T(8,128)S(1)} %copy-done.1, f32[2,512,1024]{2,1,0:T(8,128)} %all-gather.5.cloned.1.call-done, f32[512,1024]{1,0:T(8,128)} %all-reduce.3.cloned.1.call-done, pred[2]{0:T(512)(128)(4,1)S(1)} %dynamic-slice_compare_fusion), kind=kOutput, calls=%fused_computation.11 | convolution fusion | flops 6443499520 | bytes 10485762 | tf_op jit(solution)/shard_map/tak,bk->tab/dot_general | solution.py:35
  (75 shorter events, 31.1 us)
Async XLA Ops:
  7.2 81.2 %all-gather.3.cloned.1.call-start = ((), (), s32[]{:S(2)}) async-start(), calls=%async_computation | async-start | bytes 4718592 | tf_op jit(solution)/shard_map/all_gather | solution.py:22
  9.3 453.3 %all-gather.5.cloned.1.call-start = ((), (), s32[]{:S(2)}) async-start(), calls=%async_computation.1 | async-start | bytes 5242880 | tf_op jit(solution)/shard_map/all_gather | solution.py:32
  98.1 1.9 copy-start
  303.2 108.7 %copy-start.2 = (f32[2,128,1024]{2,1,0:T(8,128)S(1)}, f32[2,128,1024]{2,1,0:T(8,128)}, u32[]{:S(2)}) copy-start(f32[2,128,1024]{2,1,0:T(8,128)} %param.5) | copy-start | bytes 3145732
  420.1 9.8 %copy-start.3 = (s32[16]{0:T(128)S(1)}, s32[16]{0:T(128)}, u32[]{:S(2)}) copy-start(s32[16]{0:T(128)} %param.7) | copy-start | bytes 196
  429.7 139.0 %copy-start.1 = (f32[2,1,512,512]{3,2,1,0:T(8,128)S(1)}, f32[2,1,512,512]{3,2,1,0:T(8,128)}, u32[]{:S(2)}) copy-start(f32[2,1,512,512]{3,2,1,0:T(8,128)} %param.4) | copy-start | bytes 6291460
  429.8 138.9 %all-reduce.3.cloned.1.call-start = ((), (), s32[]{:S(2)}) async-start(), calls=%async_computation.2 | async-start | bytes 4194304 | tf_op jit(solution)/shard_map/psum | solution.py:9
Sparse Core Ops, SparseCore 0:
  10.6 77.7 all-gather.2
  429.9 32.6 all-gather.4
  466.8 101.8 all-reduce.2
where the time goes:
time: 596 us; the launch traced here: 586 us
  other arithmetic  266 us (45%)
  waiting for transfers between devices  209 us (35%)
  matrix products  50.1 us (8%)
  local copies, waits for them, and re-layouts  38.1 us (6%)
  between operations  22 us (4%)
    another operation x30, other arithmetic, per_device(): factor = jnp.linalg.cholesky(whole_diag)  172 us
    psum x1, waiting for transfers between devices, spread(): return lax.psum(block, axis)  101 us
    another operation x3, other arithmetic, solve_rows(): lax.linalg.triangular_solve(factor, flattened, left_side=False, lower=Tru...  85.5 us
    all_gather x1, waiting for transfers between devices, per_device(): whole_diag = lax.all_gather(diag_block, 'row', axis=0, tiled=True)  79 us
    all_gather x1, waiting for transfers between devices, per_device(): row_panels = lax.all_gather(own_piece, 'col', axis=1, tiled=True)  29.5 us
    another operation x24, local copies, waits for them, and re-layouts  23 us
    another operation x14, matrix products, per_device(): factor = jnp.linalg.cholesky(whole_diag)  23 us
    another operation x15, matrix products, solve_rows(): lax.linalg.triangular_solve(factor, flattened, left_side=False, lower=Tru...  16.4 us
  transfers between devices with their start and end apart: 3, of which 3 were waited for; matrix products, arithmetic and copies ran while one was open for 0% of the time, Pallas kernels for 0%

commit v1 on v0

v1 whole, which is shorter than its diff:
```python
import functools

import jax
import jax.numpy as jnp
from jax import lax
from jax.experimental import pallas as pl
from jax.experimental.pallas import tpu as pltpu
from jax.sharding import PartitionSpec as P

BLOCK = 128
WIDE = 256
F32, BF16 = jnp.float32, jnp.bfloat16


def spread_row(x, m):
    return jnp.broadcast_to(x[m : m + 1, :], x.shape)


def spread_lane(x, j):
    return jnp.broadcast_to(x[:, j : j + 1], x.shape)


def inverse_of(d):
    guess = pl.reciprocal(d, approx=True)
    return guess * (2.0 - d * guess)


def factor_block(rows_in):
    count = len(rows_in)
    work = list(rows_in)
    lane = lax.broadcasted_iota(jnp.int32, (8, BLOCK), 1)
    sub = lax.broadcasted_iota(jnp.int32, (8, BLOCK), 0)
    upper, inverse = [], []
    for b in range(count):
        o = 8 * b
        rows = [spread_row(work[b], m) for m in range(8)]
        p = {(m, l): spread_lane(rows[m], o + l) for m in range(8) for l in range(m + 1)}
        r = list(rows)
        t = [jnp.where(lane == o + m, 1.0, jnp.where(lane >= o, 0.0, rows[m])) for m in range(8)]
        f, ri = {}, []
        for j in range(8):
            ri.append(inverse_of(p[j, j]))
            for m in range(j + 1, 8):
                f[m, j] = p[m, j] * ri[j]
                for l in range(j + 1, m + 1):
                    p[m, l] = p[m, l] - f[m, j] * p[l, j]
                r[m] = r[m] - f[m, j] * r[j]
                t[m] = t[m] - f[m, j] * t[j]
        up, inv = None, None
        for m in range(8):
            s = lax.rsqrt(p[m, m])
            um, im = r[m] * s, t[m] * s
            up = um if m == 0 else jnp.where(sub == m, um, up)
            inv = im if m == 0 else jnp.where(sub == m, im, inv)
        upper.append(jnp.where(lane >= sub + o, up, 0.0))
        inverse.append(inv)
        if b + 1 < count:
            z = [None] * 8
            for m in range(7, -1, -1):
                v = jnp.where(lane < o + 8, t[m], r[m]) * ri[m]
                for l in range(7, m, -1):
                    v = v - f[l, m] * z[l]
                z[m] = v
            for i in range(b + 1, count):
                v = jnp.where((lane >= o) & (lane < o + 8), 0.0, work[i])
                for m in range(8):
                    v = v - spread_lane(work[i], o + m) * z[m]
                work[i] = v
    return upper, inverse


def dot_nt(a, b, precision=None):
    return lax.dot_general(a, b, (((1,), (1,)), ((), ())), precision=precision, preferred_element_type=F32)


def full_nt(a, b):
    return dot_nt(a, b, lax.Precision.HIGHEST)


def halves(x):
    high = x.astype(BF16)
    return high, (x - high.astype(F32)).astype(BF16)


def split_nt(ah, al, bh, bl):
    return dot_nt(ah, bh) + (dot_nt(ah, bl) + dot_nt(al, bh))


def cholesky_kernel(n_row, where_ref, *refs):
    pieces = refs[: 2 * n_row]
    own_ref, lh_ref, ll_ref, wh_ref, wl_ref, a_ref, l_ref, w_ref, s_ref, t_ref, sem = refs[2 * n_row :]
    n = a_ref.shape[0]
    count = n // BLOCK
    rows = n // n_row
    width = n // 2
    row, core = where_ref[0], where_ref[2]
    copies = []
    for i, piece in enumerate(pieces):
        source, side = row ^ (i // 2), core ^ (i % 2)
        target = a_ref.at[
            pl.ds(pl.multiple_of(source * rows, rows), rows), pl.ds(pl.multiple_of(side * width, width), width)
        ]
        copies.append(pltpu.make_async_copy(piece, target, sem.at[i]))
    for copy in copies:
        copy.start()
    for copy in copies:
        copy.wait()
    s_ref[...] = a_ref[:, 0:BLOCK]

    @pl.loop(0, count)
    def _(k):
        upper, inverse = factor_block([s_ref[8 * i : 8 * i + 8, :] for i in range(BLOCK // 8)])
        for i in range(BLOCK // 8):
            t_ref[8 * i : 8 * i + 8, :] = upper[i]
            w_ref[k, 8 * i : 8 * i + 8, :] = inverse[i]
        for step in range(count):

            @pl.when(k == step)
            def _():
                lo, hi = step * BLOCK, step * BLOCK + BLOCK
                left = n - hi
                l_ref[lo:hi, lo:hi] = t_ref[...].T
                if left:
                    l_ref[lo:hi, hi:] = jnp.zeros((BLOCK, left), F32)
                    l_ref[hi:, lo:hi] = full_nt(s_ref[BLOCK : BLOCK + left, :], w_ref[step])
                    s_ref[0:left, :] = a_ref[hi:, hi : hi + BLOCK] - full_nt(l_ref[hi:, :hi], l_ref[hi : hi + BLOCK, :hi])

    own_ref[...] = l_ref[pl.ds(pl.multiple_of(row * rows, rows), rows), :]
    lh_ref[...], ll_ref[...] = halves(l_ref[...])
    for k in range(n // WIDE):
        lo = k * WIDE
        first, second = w_ref[2 * k], w_ref[2 * k + 1]
        cross = l_ref[lo + BLOCK : lo + WIDE, lo : lo + BLOCK]
        mixed = jnp.dot(cross, first, precision=lax.Precision.HIGHEST, preferred_element_type=F32)
        corner = -jnp.dot(second, mixed, precision=lax.Precision.HIGHEST, preferred_element_type=F32)
        whole = jnp.concatenate(
            [jnp.concatenate([first, jnp.zeros_like(first)], 1), jnp.concatenate([corner, second], 1)], 0
        )
        wh_ref[k], wl_ref[k] = halves(whole)


def cholesky(where, pieces, n, n_row):
    count = n // BLOCK
    vmem, smem = pl.BlockSpec(memory_space=pltpu.VMEM), pl.BlockSpec(memory_space=pltpu.SMEM)
    return pl.pallas_call(
        functools.partial(cholesky_kernel, n_row),
        out_shape=(
            jax.ShapeDtypeStruct((n // n_row, n), F32),
            jax.ShapeDtypeStruct((n, n), BF16),
            jax.ShapeDtypeStruct((n, n), BF16),
            jax.ShapeDtypeStruct((n // WIDE, WIDE, WIDE), BF16),
            jax.ShapeDtypeStruct((n // WIDE, WIDE, WIDE), BF16),
        ),
        in_specs=[smem] + [pl.BlockSpec(memory_space=pl.ANY)] * len(pieces),
        out_specs=[vmem] * 5,
        scratch_shapes=[
            pltpu.VMEM((n, n), F32),
            pltpu.VMEM((n, n), F32),
            pltpu.VMEM((count, BLOCK, BLOCK), F32),
            pltpu.VMEM((n, BLOCK), F32),
            pltpu.VMEM((BLOCK, BLOCK), F32),
            pltpu.SemaphoreType.DMA((len(pieces),)),
        ],
        compiler_params=pltpu.CompilerParams(vmem_limit_bytes=40 * 2**20),
        cost_estimate=pl.CostEstimate(flops=8 * n**3, bytes_accessed=12 * n * n, transcendentals=0),
        name="cholesky",
    )(where, *pieces)


def solve(source, xh_ref, xl_ref, lh_ref, ll_ref, wh_ref, wl_ref, keep=None):
    n = lh_ref.shape[0]
    for k in range(n // WIDE):
        lo, hi = k * WIDE, k * WIDE + WIDE
        rest = source[:, lo:hi]
        if k:
            rest = rest - split_nt(xh_ref[:, :lo], xl_ref[:, :lo], lh_ref[lo:hi, :lo], ll_ref[lo:hi, :lo])
        rh, rl = halves(rest)
        x = split_nt(rh, rl, wh_ref[k], wl_ref[k])
        if keep is not None:
            keep(lo, hi, x)
        xh_ref[:, lo:hi], xl_ref[:, lo:hi] = halves(x)


def rows_kernel(*refs):
    n_piece = len(refs) - 9
    pieces = refs[:n_piece]
    lh_ref, ll_ref, wh_ref, wl_ref, own_ref, xh_ref, xl_ref, p_ref, sem = refs[n_piece:]
    slots, rows, n = pieces[0].shape
    copies = [pltpu.make_async_copy(piece, p_ref.at[i], sem.at[i]) for i, piece in enumerate(pieces)]
    for copy in copies:
        copy.start()

    @pl.loop(0, n_piece)
    def _(i):
        pltpu.make_async_copy(pieces[0], p_ref.at[i], sem.at[i]).wait()

        def keep(lo, hi, x):
            @pl.when(i == 0)
            def _():
                own_ref[:, :, lo:hi] = x.reshape(slots, rows, hi - lo)

        source = p_ref.at[i].reshape(slots * rows, n)
        solve(source, xh_ref.at[i], xl_ref.at[i], lh_ref, ll_ref, wh_ref, wl_ref, keep)


def factor_rows(pieces, factor):
    slots, rows, n = pieces[0].shape
    vmem = pl.BlockSpec(memory_space=pltpu.VMEM)
    count = len(pieces)
    return pl.pallas_call(
        rows_kernel,
        out_shape=(
            jax.ShapeDtypeStruct((slots, rows, n), F32),
            jax.ShapeDtypeStruct((count, slots * rows, n), BF16),
            jax.ShapeDtypeStruct((count, slots * rows, n), BF16),
        ),
        in_specs=[pl.BlockSpec(memory_space=pl.ANY)] * count + [vmem] * 4,
        out_specs=[vmem] * 3,
        scratch_shapes=[pltpu.VMEM((count, slots, rows, n), F32), pltpu.SemaphoreType.DMA((count,))],
        compiler_params=pltpu.CompilerParams(vmem_limit_bytes=40 * 2**20),
        cost_estimate=pl.CostEstimate(flops=6 * count * slots * rows * n * n, bytes_accessed=20 * n * n, transcendentals=0),
        name="factor_rows",
    )(*pieces, *factor)


def update_kernel(n_piece, where_ref, p_ref, lh_ref, ll_ref, wh_ref, wl_ref, xh_ref, xl_ref, t_ref, out_ref, ch_ref, cl_ref):
    slots, _, tile, _ = t_ref.shape
    rows = tile // n_piece
    col = where_ref[1]
    solve(p_ref, ch_ref, cl_ref, lh_ref, ll_ref, wh_ref, wl_ref)

    @pl.loop(0, n_piece)
    def _(i):
        at = pl.ds(pl.multiple_of((col ^ i) * rows, rows), rows)
        product = split_nt(xh_ref[i], xl_ref[i], ch_ref[...], cl_ref[...])
        for s in range(slots):
            live = where_ref[3 + s] > 0
            new = t_ref[s, 0, at, :] - product[s * rows : (s + 1) * rows]
            out_ref[s, 0, at, :] = jnp.where(live, new, jnp.zeros_like(new))


def update(where, column, factor, xh, xl, trailing):
    tile, n = column.shape
    vmem, smem = pl.BlockSpec(memory_space=pltpu.VMEM), pl.BlockSpec(memory_space=pltpu.SMEM)
    return pl.pallas_call(
        functools.partial(update_kernel, xh.shape[0]),
        out_shape=jax.ShapeDtypeStruct(trailing.shape, F32),
        in_specs=[smem] + [vmem] * 8,
        out_specs=vmem,
        scratch_shapes=[pltpu.VMEM((tile, n), BF16), pltpu.VMEM((tile, n), BF16)],
        compiler_params=pltpu.CompilerParams(vmem_limit_bytes=40 * 2**20),
        cost_estimate=pl.CostEstimate(flops=10 * tile * n * n, bytes_accessed=20 * n * n, transcendentals=0),
        name="update",
    )(where, column, *factor, xh, xl, trailing)


def flip(x, axis, size, bit):
    return lax.ppermute(x, axis, [(i, i ^ bit) for i in range(size)])


def gather_flips(x, axis, size):
    found = {0: x}
    bit = size // 2
    while bit:
        for p in list(found):
            found[p | bit] = flip(found[p], axis, size, bit)
        bit //= 2
    return [found[p] for p in range(size)]


def per_device(n_row, n_col, trailing, panel_block, diag_block, tile_map):
    slots, rows, n = panel_block.shape
    tile = rows * n_col
    row, col = lax.axis_index("row"), lax.axis_index("col")
    slot_index = jnp.arange(tile_map.shape[0], dtype=jnp.int32)
    own_tiles = lax.dynamic_slice_in_dim(tile_map, row * slots, slots)
    live = (own_tiles >= col).astype(jnp.int32)
    where = jnp.concatenate([jnp.stack([row, col, col & 1]).astype(jnp.int32), live])

    side = lax.dynamic_slice_in_dim(diag_block, (col & 1) * (n // 2), n // 2, 1)
    other = lax.dynamic_slice_in_dim(diag_block, (1 - (col & 1)) * (n // 2), n // 2, 1)
    mine = gather_flips(side, "row", n_row)
    theirs = [other] + [flip(x, "col", n_col, 1) for x in mine[1:]]
    diag_pieces = [x for pair in zip(mine, theirs) for x in pair]

    row_pieces = gather_flips(panel_block, "col", n_col)

    chunk = rows // n_row
    parts = panel_block.reshape(slots, n_row, chunk, n).transpose(1, 0, 2, 3)
    parts = lax.all_to_all(parts, "row", 0, 0, tiled=True).reshape(n_row * slots, chunk, n)
    chosen = []
    for c in range(n_col):
        slot = jnp.sum(jnp.where(tile_map == c, slot_index, 0))
        chosen.append(lax.dynamic_index_in_dim(parts, slot, 0, keepdims=False))
    own_column = lax.all_to_all(jnp.stack(chosen), "col", 0, 0, tiled=True)
    chunks = jnp.stack(gather_flips(own_column, "row", n_row))
    order = jnp.arange(n_row, dtype=jnp.int32) ^ row
    column = chunks[order].transpose(1, 0, 2, 3).reshape(tile, n)

    diag_factor, *factor = cholesky(where, diag_pieces, n, n_row)
    panel_factor, xh, xl = factor_rows(row_pieces, factor)
    updated = update(where, column, factor, xh, xl, trailing)
    return updated, panel_factor, diag_factor


def solution(mesh):
    n_row, n_col = mesh.shape["row"], mesh.shape["col"]
    in_specs = (P("row", "col", None, None), P("row", "col", None), P("row", None), P())
    out_specs = (P("row", "col", None, None), P("row", "col", None), P("row", None))
    return jax.shard_map(
        functools.partial(per_device, n_row, n_col),
        mesh=mesh,
        in_specs=in_specs,
        out_specs=out_specs,
        check_vma=False,
    )
```

time: 596 us -> 215 us (0.36); the launches traced: 586 us -> 214 us
  other arithmetic: 266 us -> 1.62 us
  waiting for transfers between devices: 209 us -> 53.2 us
  Pallas kernels: 0 us -> 82.6 us
  matrix products: 50.1 us -> 0 us
  starting transfers between devices: 0.12 us -> 34.8 us
  between operations: 22 us -> 8.36 us
    another operation x33 -> x1, other arithmetic: 258 us -> 0.72 us  [per_device(): own_column = lax.all_to_all(jnp.stack(chosen), 'col', 0, 0, tiled=True)]
    all_gather x2 -> x0, waiting for transfers between devices: 109 us -> none  [the longest x1 79 us: per_device(): whole_diag = lax.all_gather(diag_block, 'row', axis=0, tiled=True)]
    psum x1 -> x0, waiting for transfers between devices: 101 us -> none  [spread(): return lax.psum(block, axis)]
    pallas_call x0 -> x3, Pallas kernels: none -> 82.6 us  [the longest x1 59.5 us: cholesky(): pl.pallas_call(functools.partial(cholesky_kernel, n_row), out_shape=(jax....]
    ppermute x0 -> x24, waiting for transfers between devices: none -> 53.2 us  [flip(): return lax.ppermute(x, axis, [(i, i ^ bit) for i in range(size)])]
    another operation x29 -> x0, matrix products: 39.4 us -> none  [the longest x14 23 us: per_device(): factor = jnp.linalg.cholesky(whole_diag)]
    another operation x33 -> x1, local copies, waits for them, and re-layouts: 25.6 us -> 0.72 us  [per_device(): chunks = jnp.stack(gather_flips(own_column, 'row', n_row))]
    ppermute x0 -> x24, starting transfers between devices: none -> 23.4 us  [flip(): return lax.ppermute(x, axis, [(i, i ^ bit) for i in range(size)])]
  transfers between devices with their start and end apart: 3 -> 26, of which waited for: 3 -> 8; matrix products, arithmetic and copies ran while one was open for 0% -> 4% of each run, Pallas kernels for 0% -> 34%
where the time goes in v1:
time: 215 us; the launch traced here: 214 us
  Pallas kernels  82.6 us (38%)
  waiting for transfers between devices  53.2 us (25%)
  starting transfers between devices  34.8 us (16%)
  local copies, waits for them, and re-layouts  33.7 us (16%)
  between operations  8.36 us (4%)
    pallas_call x1, Pallas kernels, cholesky(): pl.pallas_call(functools.partial(cholesky_kernel, n_row), out_shape=(jax....  59.5 us
    ppermute x24, waiting for transfers between devices, flip(): return lax.ppermute(x, axis, [(i, i ^ bit) for i in range(size)])  53.2 us
    unnamed x45, local copies, waits for them, and re-layouts  24 us
    ppermute x24, starting transfers between devices, flip(): return lax.ppermute(x, axis, [(i, i ^ bit) for i in range(size)])  23.4 us
    pallas_call x1, Pallas kernels, factor_rows(): pl.pallas_call(rows_kernel, out_shape=(jax.ShapeDtypeStruct((slots, rows,...  13 us
    pallas_call x1, Pallas kernels, update(): pl.pallas_call(functools.partial(update_kernel, xh.shape[0]), out_shape=j...  9.97 us
    all_to_all x1, starting transfers between devices, per_device(): lax.all_to_all(parts, 'row', 0, 0, tiled=True)  7.38 us
  transfers between devices with their start and end apart: 26, of which 8 were waited for; matrix products, arithmetic and copies ran while one was open for 4% of the time, Pallas kernels for 34%

profile of v1, /device:TPU:0, one launch (start us, length us, event | category | flops | bytes accessed | tf_op | source)
XLA Modules:
  0.0 214.3 jit_solution(7362880541723925077)
XLA Ops:
  0.6 2.4 %copy.10 = f32[8,2,16,1024]{3,2,1,0:T(8,128)} copy(f32[8,2,16,1024]{3,2,0,1:T(8,128)} %bitcast.28) | data formatting | bytes 2097152 | tf_op jit(solution)/shard_map/transpose | solution.py:289
  3.0 7.4 %all-to-all-start = ((f32[8,2,16,1024]{3,2,1,0:T(8,128)}), f32[8,2,16,1024]{3,2,1,0:T(8,128)}, u32[]{:S(2)}, u32[]{:S(2)}) async-start(f32[8,2,16,1024]{3,2,1,0:T(8,128)} %copy.10), calls=%async_computation | async-start | bytes 2097152 | tf_op jit(solution)/shard_map/all_to_all | solution.py:290
  10.4 3.0 %collective-permute-start.13 = (f32[128,512]{1,0:T(8,128)S(1)}, f32[128,512]{1,0:T(8,128)S(1)}, u32[]{:S(2)}, u32[]{:S(2)}) collective-permute-start(f32[128,512]{1,0:T(8,128)S(1)} %get-tuple-element.28.refs_0_), channel_id=1, source_target_pairs={{0,16},{4,20},{8,24},{12,28},{16,0},{20,4},{24,8},{28,12},{1,17},{... | collective-permute-start | bytes 786440 | tf_op jit(solution)/shard_map/ppermute | solution.py:258
  13.4 1.5 collective-permute-start.9
  14.9 1.5 collective-permute-start.22
  16.4 1.5 collective-permute-start.7
  17.9 29.5 %collective-permute-done.13.refs_8_ = f32[128,512]{1,0:T(8,128)S(1)} collective-permute-done((f32[128,512]{1,0:T(8,128)S(1)}, f32[128,512]{1,0:T(8,128)S(1)}, u32[]{:S(2)}, u32[]{:S(2)}) %collective-permute-start.13) | collective-permute-done | bytes 262176 | tf_op jit(solution)/shard_map/ppermute | solution.py:258
  47.4 1.4 collective-permute-start.15
  49.4 5.0 %collective-permute-done.17.refs_12_ = f32[128,512]{1,0:T(8,128)} collective-permute-done((f32[128,512]{1,0:T(8,128)S(1)}, f32[128,512]{1,0:T(8,128)}, u32[]{:S(2)}, u32[]{:S(2)}) %collective-permute-start.17) | collective-permute-done | bytes 262176 | tf_op jit(solution)/shard_map/ppermute | solution.py:258
  54.4 2.3 %collective-permute-done.15.refs_10_ = f32[128,512]{1,0:T(8,128)} collective-permute-done((f32[128,512]{1,0:T(8,128)S(1)}, f32[128,512]{1,0:T(8,128)}, u32[]{:S(2)}, u32[]{:S(2)}) %collective-permute-start.15) | collective-permute-done | bytes 262176 | tf_op jit(solution)/shard_map/ppermute | solution.py:258
  56.8 3.3 %collective-permute-done.11.refs_6_ = f32[128,512]{1,0:T(8,128)} collective-permute-done((f32[128,512]{1,0:T(8,128)S(1)}, f32[128,512]{1,0:T(8,128)}, u32[]{:S(2)}, u32[]{:S(2)}) %collective-permute-start.11) | collective-permute-done | bytes 262176 | tf_op jit(solution)/shard_map/ppermute | solution.py:258
  60.1 1.7 collective-permute-start.19
  61.8 0.7 fusion
  63.2 3.5 %collective-permute-done.19.refs_14_ = f32[128,512]{1,0:T(8,128)} collective-permute-done((f32[128,512]{1,0:T(8,128)}, f32[128,512]{1,0:T(8,128)}, u32[]{:S(2)}, u32[]{:S(2)}) %collective-permute-start.19) | collective-permute-done | bytes 262176 | tf_op jit(solution)/shard_map/ppermute | solution.py:258
  74.4 1.0 constant_dynamic-slice_fusion.5
  76.8 4.0 %all-to-all-start.1 = ((f32[4,16,1024]{2,1,0:T(8,128)}), f32[4,16,1024]{2,1,0:T(8,128)}, u32[]{:S(2)}, u32[]{:S(2)}) async-start(f32[4,16,1024]{2,1,0:T(8,128)} %pad_maximum_fusion), calls=%async_computation.1 | async-start | bytes 524288 | tf_op jit(solution)/shard_map/all_to_all | solution.py:295
  80.8 59.5 %cholesky.1 = (f32[128,1024]{1,0:T(8,128)}, bf16[1024,1024]{1,0:T(8,128)(2,1)S(1)}, bf16[1024,1024]{1,0:T(8,128)(2,1)S(1)}, bf16[4,256,256]{2,1,0:T(8,128)(2,1)S(1)}, bf16[4,256,256]{2,1,0:T(8,128)(2,1)S(1)}) custom-call(s32[5]{0:T(128)S(1)} %pad_add_fusion.where_ref, f32[128,512]{1,0:T(8,128)S(1)} %get-tuple-element.28.refs_0_, ...), custom_call_target="tpu_custom_call" | custom-call | flops 8589934592 | bytes 12582912 | tf_op jit(solution)/shard_map/cholesky/pallas_call | solution.py:145
  140.4 1.3 copy-done.2
  141.8 1.3 copy-done.5
  143.1 0.8 copy-done.12
  143.9 0.8 copy-done.15
  144.7 1.7 collective-permute-start
  146.4 1.8 collective-permute-start.1
  148.2 2.3 %collective-permute-start.3 = (f32[4,16,1024]{2,1,0:T(8,128)}, f32[4,16,1024]{2,1,0:T(8,128)S(1)}, u32[]{:S(2)}, u32[]{:S(2)}) collective-permute-start(f32[4,16,1024]{2,1,0:T(8,128)} %all-to-all-done.1), channel_id=1, source_target_pairs={{0,16},{4,20},{8,24},{12,28},{16,0},{20,4},{24,8},{28,12},{1,17},{... | collective-permute-start | bytes 786440 | tf_op jit(solution)/shard_map/ppermute | solution.py:258
  150.4 1.7 bitcast_dynamic-update-slice_fusion.7
  152.1 1.6 copy-done.3
  153.7 1.6 copy-done.6
  155.3 1.0 copy-done.13
  156.4 1.0 copy-done.16
  157.4 13.0 %factor_rows.1 = (f32[2,128,1024]{2,1,0:T(8,128)}, bf16[4,256,1024]{2,1,0:T(8,128)(2,1)S(1)}, bf16[4,256,1024]{2,1,0:T(8,128)(2,1)S(1)}) custom-call(f32[2,128,1024]{2,1,0:T(8,128)S(1)} %copy-done, f32[2,128,1024]{2,1,0:T(8,128)} %collective-permute-done.21.refs_1_, f32[2,128,1024]{2,1,0:T(8,128)S(1)} %collective-permute-done.22.refs_2_, ...), custom_call_target="tpu_custom_call" | custom-call | flops 6442450944 | bytes 20971520 | tf_op jit(solution)/shard_map/factor_rows/pallas_call | solution.py:210
  170.5 1.4 copy-done.8
  171.8 1.4 copy-done.10
  173.5 1.4 collective-permute-start.5
  174.9 1.7 collective-permute-start.2
  178.1 2.9 %collective-permute-done.5 = f32[4,16,1024]{2,1,0:T(8,128)S(1)} collective-permute-done((f32[4,16,1024]{2,1,0:T(8,128)S(1)}, f32[4,16,1024]{2,1,0:T(8,128)S(1)}, u32[]{:S(2)}, u32[]{:S(2)}) %collective-permute-start.5) | collective-permute-done | bytes 262176 | tf_op jit(solution)/shard_map/ppermute | solution.py:258
  181.1 1.7 collective-permute-start.6
  182.8 5.3 %collective-permute-done.2 = f32[4,16,1024]{2,1,0:T(8,128)S(1)} collective-permute-done((f32[4,16,1024]{2,1,0:T(8,128)S(1)}, f32[4,16,1024]{2,1,0:T(8,128)S(1)}, u32[]{:S(2)}, u32[]{:S(2)}) %collective-permute-start.2) | collective-permute-done | bytes 262176 | tf_op jit(solution)/shard_map/ppermute | solution.py:258
  188.1 0.7 bitcast_dynamic-update-slice_fusion.4
  189.5 0.7 bitcast_dynamic-update-slice_fusion.2
  190.3 0.7 bitcast_dynamic-update-slice_fusion.1
  191.0 1.3 collective-permute-done.6
  192.3 0.7 bitcast_dynamic-update-slice_fusion
  193.0 3.7 %gather_fusion = f32[8,4,16,1024]{3,2,1,0:T(8,128)} fusion(f32[8,4,16,1024]{3,2,1,0:T(8,128)} %bitcast_dynamic-update-slice_fusion, s32[1024]{0:T(1024)S(1)} %pad_clamp_fusion), kind=kCustom, calls=%fused_computation | custom fusion | bytes 4194336 | tf_op jit(solution)/shard_map/gather | solution.py:298
  196.7 2.0 copy.11
  199.6 1.6 copy-done.7
  201.2 1.6 copy-done.9
  202.7 1.6 copy-done.11
  204.3 10.0 %update.1 = f32[2,1,512,512]{3,2,1,0:T(8,128)} custom-call(s32[5]{0:T(128)S(1)} %pad_add_fusion.where_ref, f32[512,1024]{1,0:T(8,128)S(1)} %bitcast.27, bf16[1024,1024]{1,0:T(8,128)(2,1)S(1)} %copy-done.4, bf16[1024,1024]{1,0:T(8,128)(2,1)S(1)} %copy-done.7, bf16[4,256,256]{2,1,0:T(8,128)(2,1)S(1)} %copy-done.14, bf16[4,256,256]{2,1,0:T(8,128)(2,1)S(1)} %copy-done.16, ...), custom_call_target="tpu_custom_call" | custom-call | flops 5368709120 | bytes 20971520 | tf_op jit(solution)/shard_map/update/pallas_call | solution.py:245
  (64 shorter events, 6.2 us)
Async XLA Ops:
  0.6 9.8 %copy-start.17 = (f32[128,1024]{1,0:T(8,128)S(1)}, f32[128,1024]{1,0:T(8,128)}, u32[]{:S(2)}) copy-start(f32[128,1024]{1,0:T(8,128)} %param.6) | copy-start | bytes 1572868
  3.0 11.9 %copy-start = (f32[2,128,1024]{2,1,0:T(8,128)S(1)}, f32[2,128,1024]{2,1,0:T(8,128)}, u32[]{:S(2)}) copy-start(f32[2,128,1024]{2,1,0:T(8,128)} %refs_0_.1) | copy-start | bytes 3145732
  3.0 58.8 %copy-start.18 = (s32[16]{0:T(128)S(1)}, s32[16]{0:T(128)}, u32[]{:S(2)}) copy-start(s32[16]{0:T(128)} %param.7) | copy-start | bytes 196
  3.0 71.4 %all-to-all-start = ((f32[8,2,16,1024]{3,2,1,0:T(8,128)}), f32[8,2,16,1024]{3,2,1,0:T(8,128)}, u32[]{:S(2)}, u32[]{:S(2)}) async-start(f32[8,2,16,1024]{3,2,1,0:T(8,128)} %copy.10), calls=%async_computation | async-start | bytes 2097152 | tf_op jit(solution)/shard_map/all_to_all | solution.py:290
  10.4 36.9 %collective-permute-start.13 = (f32[128,512]{1,0:T(8,128)S(1)}, f32[128,512]{1,0:T(8,128)S(1)}, u32[]{:S(2)}, u32[]{:S(2)}) collective-permute-start(f32[128,512]{1,0:T(8,128)S(1)} %get-tuple-element.28.refs_0_), channel_id=1, source_target_pairs={{0,16},{4,20},{8,24},{12,28},{16,0},{20,4},{24,8},{28,12},{1,17},{... | collective-permute-start | bytes 786440 | tf_op jit(solution)/shard_map/ppermute | solution.py:258
  13.4 35.4 %collective-permute-start.9 = (f32[128,512]{1,0:T(8,128)S(1)}, f32[128,512]{1,0:T(8,128)S(1)}, u32[]{:S(2)}, u32[]{:S(2)}) collective-permute-start(f32[128,512]{1,0:T(8,128)S(1)} %get-tuple-element.28.refs_0_), channel_id=1, source_target_pairs={{0,8},{4,12},{8,0},{12,4},{16,24},{20,28},{24,16},{28,20},{1,9},{5... | collective-permute-start | bytes 786440 | tf_op jit(solution)/shard_map/ppermute | solution.py:258
  14.9 61.1 %collective-permute-start.22 = (f32[2,128,1024]{2,1,0:T(8,128)S(1)}, f32[2,128,1024]{2,1,0:T(8,128)S(1)}, u32[]{:S(2)}, u32[]{:S(2)}) collective-permute-start(f32[2,128,1024]{2,1,0:T(8,128)S(1)} %copy-done), channel_id=1, source_target_pairs={{0,2},{1,3},{2,0},{3,1},{4,6},{5,7},{6,4},{7,5},{8,10},{9,11},{10,... | collective-permute-start | bytes 3145736 | tf_op jit(solution)/shard_map/ppermute | solution.py:258
  16.4 33.0 %collective-permute-start.7 = (f32[128,512]{1,0:T(8,128)S(1)}, f32[128,512]{1,0:T(8,128)S(1)}, u32[]{:S(2)}, u32[]{:S(2)}) collective-permute-start(f32[128,512]{1,0:T(8,128)S(1)} %get-tuple-element.28.refs_0_), channel_id=1, source_target_pairs={{0,4},{4,0},{8,12},{12,8},{16,20},{20,16},{24,28},{28,24},{1,5},{5... | collective-permute-start | bytes 786440 | tf_op jit(solution)/shard_map/ppermute | solution.py:258
  47.4 7.0 %collective-permute-start.17 = (f32[128,512]{1,0:T(8,128)S(1)}, f32[128,512]{1,0:T(8,128)}, u32[]{:S(2)}, u32[]{:S(2)}) collective-permute-start(f32[128,512]{1,0:T(8,128)S(1)} %collective-permute-done.13.refs_8_), channel_id=1, source_target_pairs={{0,8},{4,12},{8,0},{12,4},{16,24},{20,28},{24,16},{28,20},{1,9},{5... | collective-permute-start | bytes 786440 | tf_op jit(solution)/shard_map/ppermute | solution.py:258
  47.4 9.4 %collective-permute-start.15 = (f32[128,512]{1,0:T(8,128)S(1)}, f32[128,512]{1,0:T(8,128)}, u32[]{:S(2)}, u32[]{:S(2)}) collective-permute-start(f32[128,512]{1,0:T(8,128)S(1)} %collective-permute-done.13.refs_8_), channel_id=1, source_target_pairs={{0,4},{4,0},{8,12},{12,8},{16,20},{20,16},{24,28},{28,24},{1,5},{5... | collective-permute-start | bytes 786440 | tf_op jit(solution)/shard_map/ppermute | solution.py:258
  48.8 11.2 %collective-permute-start.11 = (f32[128,512]{1,0:T(8,128)S(1)}, f32[128,512]{1,0:T(8,128)}, u32[]{:S(2)}, u32[]{:S(2)}) collective-permute-start(f32[128,512]{1,0:T(8,128)S(1)} %collective-permute-done.9.refs_4_), channel_id=1, source_target_pairs={{0,4},{4,0},{8,12},{12,8},{16,20},{20,16},{24,28},{28,24},{1,5},{5... | collective-permute-start | bytes 786440 | tf_op jit(solution)/shard_map/ppermute | solution.py:258
  49.4 13.1 %collective-permute-start.14 = (f32[128,512]{1,0:T(8,128)S(1)}, f32[128,512]{1,0:T(8,128)}, u32[]{:S(2)}, u32[]{:S(2)}) collective-permute-start(f32[128,512]{1,0:T(8,128)S(1)} %collective-permute-done.13.refs_8_), channel_id=1, source_target_pairs={{0,1},{1,0},{2,3},{3,2},{4,5},{5,4},{6,7},{7,6},{8,9},{9,8},{10,11... | collective-permute-start | bytes 786440 | tf_op jit(solution)/shard_map/ppermute | solution.py:258
  54.4 8.2 %collective-permute-start.10 = (f32[128,512]{1,0:T(8,128)S(1)}, f32[128,512]{1,0:T(8,128)}, u32[]{:S(2)}, u32[]{:S(2)}) collective-permute-start(f32[128,512]{1,0:T(8,128)S(1)} %collective-permute-done.9.refs_4_), channel_id=1, source_target_pairs={{0,1},{1,0},{2,3},{3,2},{4,5},{5,4},{6,7},{7,6},{8,9},{9,8},{10,11... | collective-permute-start | bytes 786440 | tf_op jit(solution)/shard_map/ppermute | solution.py:258
  56.8 6.4 %collective-permute-start.8 = (f32[128,512]{1,0:T(8,128)S(1)}, f32[128,512]{1,0:T(8,128)}, u32[]{:S(2)}, u32[]{:S(2)}) collective-permute-start(f32[128,512]{1,0:T(8,128)S(1)} %collective-permute-done.7.refs_2_), channel_id=1, source_target_pairs={{0,1},{1,0},{2,3},{3,2},{4,5},{5,4},{6,7},{7,6},{8,9},{9,8},{10,11... | collective-permute-start | bytes 786440 | tf_op jit(solution)/shard_map/ppermute | solution.py:258
  60.1 6.7 %collective-permute-start.19 = (f32[128,512]{1,0:T(8,128)}, f32[128,512]{1,0:T(8,128)}, u32[]{:S(2)}, u32[]{:S(2)}) collective-permute-start(f32[128,512]{1,0:T(8,128)} %collective-permute-done.17.refs_12_), channel_id=1, source_target_pairs={{0,4},{4,0},{8,12},{12,8},{16,20},{20,16},{24,28},{28,24},{1,5},{5... | collective-permute-start | bytes 786440 | tf_op jit(solution)/shard_map/ppermute | solution.py:258
  62.6 12.8 %collective-permute-start.18 = (f32[128,512]{1,0:T(8,128)}, f32[128,512]{1,0:T(8,128)}, u32[]{:S(2)}, u32[]{:S(2)}) collective-permute-start(f32[128,512]{1,0:T(8,128)} %collective-permute-done.17.refs_12_), channel_id=1, source_target_pairs={{0,1},{1,0},{2,3},{3,2},{4,5},{5,4},{6,7},{7,6},{8,9},{9,8},{10,11... | collective-permute-start | bytes 786440 | tf_op jit(solution)/shard_map/ppermute | solution.py:258
  62.6 18.2 %collective-permute-start.16 = (f32[128,512]{1,0:T(8,128)}, f32[128,512]{1,0:T(8,128)}, u32[]{:S(2)}, u32[]{:S(2)}) collective-permute-start(f32[128,512]{1,0:T(8,128)} %collective-permute-done.15.refs_10_), channel_id=1, source_target_pairs={{0,1},{1,0},{2,3},{3,2},{4,5},{5,4},{6,7},{7,6},{8,9},{9,8},{10,11... | collective-permute-start | bytes 786440 | tf_op jit(solution)/shard_map/ppermute | solution.py:258
  63.2 17.7 %collective-permute-start.12 = (f32[128,512]{1,0:T(8,128)}, f32[128,512]{1,0:T(8,128)}, u32[]{:S(2)}, u32[]{:S(2)}) collective-permute-start(f32[128,512]{1,0:T(8,128)} %collective-permute-done.11.refs_6_), channel_id=1, source_target_pairs={{0,1},{1,0},{2,3},{3,2},{4,5},{5,4},{6,7},{7,6},{8,9},{9,8},{10,11... | collective-permute-start | bytes 786440 | tf_op jit(solution)/shard_map/ppermute | solution.py:258
  66.8 14.1 %collective-permute-start.20 = (f32[128,512]{1,0:T(8,128)}, f32[128,512]{1,0:T(8,128)}, u32[]{:S(2)}, u32[]{:S(2)}) collective-permute-start(f32[128,512]{1,0:T(8,128)} %collective-permute-done.19.refs_14_), channel_id=1, source_target_pairs={{0,1},{1,0},{2,3},{3,2},{4,5},{5,4},{6,7},{7,6},{8,9},{9,8},{10,11... | collective-permute-start | bytes 786440 | tf_op jit(solution)/shard_map/ppermute | solution.py:258
  75.4 76.7 %collective-permute-start.21 = (f32[2,128,1024]{2,1,0:T(8,128)S(1)}, f32[2,128,1024]{2,1,0:T(8,128)}, u32[]{:S(2)}, u32[]{:S(2)}) collective-permute-start(f32[2,128,1024]{2,1,0:T(8,128)S(1)} %copy-done), channel_id=1, source_target_pairs={{0,1},{1,0},{2,3},{3,2},{4,5},{5,4},{6,7},{7,6},{8,9},{9,8},{10,11... | collective-permute-start | bytes 3145736 | tf_op jit(solution)/shard_map/ppermute | solution.py:258
  76.0 76.2 %collective-permute-start.23 = (f32[2,128,1024]{2,1,0:T(8,128)S(1)}, f32[2,128,1024]{2,1,0:T(8,128)}, u32[]{:S(2)}, u32[]{:S(2)}) collective-permute-start(f32[2,128,1024]{2,1,0:T(8,128)S(1)} %collective-permute-done.22.refs_2_), channel_id=1, source_target_pairs={{0,1},{1,0},{2,3},{3,2},{4,5},{5,4},{6,7},{7,6},{8,9},{9,8},{10,11... | collective-permute-start | bytes 3145736 | tf_op jit(solution)/shard_map/ppermute | solution.py:258
  76.8 67.9 %all-to-all-start.1 = ((f32[4,16,1024]{2,1,0:T(8,128)}), f32[4,16,1024]{2,1,0:T(8,128)}, u32[]{:S(2)}, u32[]{:S(2)}) async-start(f32[4,16,1024]{2,1,0:T(8,128)} %pad_maximum_fusion), calls=%async_computation.1 | async-start | bytes 524288 | tf_op jit(solution)/shard_map/all_to_all | solution.py:295
  140.4 1.4 copy-start.2
  141.8 1.3 copy-start.5
  143.1 0.8 copy-start.12
  143.9 0.8 copy-start.15
  144.7 32.0 %collective-permute-start = (f32[4,16,1024]{2,1,0:T(8,128)}, f32[4,16,1024]{2,1,0:T(8,128)S(1)}, u32[]{:S(2)}, u32[]{:S(2)}) collective-permute-start(f32[4,16,1024]{2,1,0:T(8,128)} %all-to-all-done.1), channel_id=1, source_target_pairs={{0,4},{4,0},{8,12},{12,8},{16,20},{20,16},{24,28},{28,24},{1,5},{5... | collective-permute-start | bytes 786440 | tf_op jit(solution)/shard_map/ppermute | solution.py:258
  146.4 28.5 %collective-permute-start.1 = (f32[4,16,1024]{2,1,0:T(8,128)}, f32[4,16,1024]{2,1,0:T(8,128)S(1)}, u32[]{:S(2)}, u32[]{:S(2)}) collective-permute-start(f32[4,16,1024]{2,1,0:T(8,128)} %all-to-all-done.1), channel_id=1, source_target_pairs={{0,8},{4,12},{8,0},{12,4},{16,24},{20,28},{24,16},{28,20},{1,9},{5... | collective-permute-start | bytes 786440 | tf_op jit(solution)/shard_map/ppermute | solution.py:258
  148.2 25.1 %collective-permute-start.3 = (f32[4,16,1024]{2,1,0:T(8,128)}, f32[4,16,1024]{2,1,0:T(8,128)S(1)}, u32[]{:S(2)}, u32[]{:S(2)}) collective-permute-start(f32[4,16,1024]{2,1,0:T(8,128)} %all-to-all-done.1), channel_id=1, source_target_pairs={{0,16},{4,20},{8,24},{12,28},{16,0},{20,4},{24,8},{28,12},{1,17},{... | collective-permute-start | bytes 786440 | tf_op jit(solution)/shard_map/ppermute | solution.py:258
  152.1 1.6 copy-start.3
  153.7 1.6 copy-start.6
  155.3 1.0 copy-start.13
  156.4 1.0 copy-start.16
  170.4 1.4 copy-start.8
  171.8 1.4 copy-start.10
  173.2 16.3 %collective-permute-start.4 = (f32[4,16,1024]{2,1,0:T(8,128)S(1)}, f32[4,16,1024]{2,1,0:T(8,128)S(1)}, u32[]{:S(2)}, u32[]{:S(2)}) collective-permute-start(f32[4,16,1024]{2,1,0:T(8,128)S(1)} %collective-permute-done.3), channel_id=1, source_target_pairs={{0,4},{4,0},{8,12},{12,8},{16,20},{20,16},{24,28},{28,24},{1,5},{5... | collective-permute-start | bytes 786440 | tf_op jit(solution)/shard_map/ppermute | solution.py:258
  173.5 7.5 %collective-permute-start.5 = (f32[4,16,1024]{2,1,0:T(8,128)S(1)}, f32[4,16,1024]{2,1,0:T(8,128)S(1)}, u32[]{:S(2)}, u32[]{:S(2)}) collective-permute-start(f32[4,16,1024]{2,1,0:T(8,128)S(1)} %collective-permute-done.3), channel_id=1, source_target_pairs={{0,8},{4,12},{8,0},{12,4},{16,24},{20,28},{24,16},{28,20},{1,9},{5... | collective-permute-start | bytes 786440 | tf_op jit(solution)/shard_map/ppermute | solution.py:258
  174.9 13.1 %collective-permute-start.2 = (f32[4,16,1024]{2,1,0:T(8,128)S(1)}, f32[4,16,1024]{2,1,0:T(8,128)S(1)}, u32[]{:S(2)}, u32[]{:S(2)}) collective-permute-start(f32[4,16,1024]{2,1,0:T(8,128)S(1)} %collective-permute-done.1), channel_id=1, source_target_pairs={{0,4},{4,0},{8,12},{12,8},{16,20},{20,16},{24,28},{28,24},{1,5},{5... | collective-permute-start | bytes 786440 | tf_op jit(solution)/shard_map/ppermute | solution.py:258
  181.1 11.2 %collective-permute-start.6 = (f32[4,16,1024]{2,1,0:T(8,128)S(1)}, f32[4,16,1024]{2,1,0:T(8,128)S(1)}, u32[]{:S(2)}, u32[]{:S(2)}) collective-permute-start(f32[4,16,1024]{2,1,0:T(8,128)S(1)} %collective-permute-done.5), channel_id=1, source_target_pairs={{0,4},{4,0},{8,12},{12,8},{16,20},{20,16},{24,28},{28,24},{1,5},{5... | collective-permute-start | bytes 786440 | tf_op jit(solution)/shard_map/ppermute | solution.py:258
  193.0 5.7 %copy-start.14 = (bf16[4,256,256]{2,1,0:T(8,128)(2,1)S(1)}, bf16[4,256,256]{2,1,0:T(8,128)(2,1)}, u32[]{:S(2)}) copy-start(bf16[4,256,256]{2,1,0:T(8,128)(2,1)} %copy-done.12) | copy-start | bytes 1572868
  196.7 2.2 %copy-start.1 = (f32[2,1,512,512]{3,2,1,0:T(8,128)S(1)}, f32[2,1,512,512]{3,2,1,0:T(8,128)}, u32[]{:S(2)}) copy-start(f32[2,1,512,512]{3,2,1,0:T(8,128)} %t_ref.1) | copy-start | bytes 6291460
  196.7 2.9 %copy-start.4 = (bf16[1024,1024]{1,0:T(8,128)(2,1)S(1)}, bf16[1024,1024]{1,0:T(8,128)(2,1)}, u32[]{:S(2)}) copy-start(bf16[1024,1024]{1,0:T(8,128)(2,1)} %copy-done.2) | copy-start | bytes 6291460
  199.6 1.6 copy-start.7
  201.2 1.6 copy-start.9
  202.7 1.6 copy-start.11
